TPU v7x, 256 devices: a whole 4x4x8 slice. The times are simulated.
256 devices in a mesh: tok: 32 (over z_hi, y, core), voc: 8 (over x, z_lo).
Axes of the slice: x: 4, y: 4, z: 8 (z_hi: 4, z_lo: 2; z = z_hi * 2 + z_lo), core: 2. Of those that a mesh axis runs over, the one named last changes fastest.
Arguments:
- hidden: bfloat16 [12288, 2304], P('tok'), may hold values from -6 to 6
- head: bfloat16 [2304, 16000], P(None, 'voc'), may hold values from -0.375 to 0.375
- teacher_logp: bfloat16 [12288, 16000], P('tok', 'voc'), may hold values from -30 to 0
- slot_blocks: int32 [128], replicated, may hold values from 0 to 127, as said below
- segment_ids: int32 [12288], P('tok'), may hold values from 0 to 63, never falling along the last dimension, each value on 1 to 768 neighbouring positions
Outputs:
- d_hidden: bfloat16 [12288, 2304], P('tok', 'voc')
- d_head: float32 [2304, 16000], P('tok', 'voc')
Inputs may be any that keep to these rules, and one draw needn't show every extreme that they name: `slot_blocks`: each of the 128 blocks is named exactly once; the 16 entries of teacher voc index j (entries j * 16 to (j + 1) * 16 - 1) name exactly 2 blocks of the range k * 16 to (k + 1) * 16 - 1 for every voc index k. `segment_ids`: never falling along the tokens; each of the 64 segments has 1 to 768 tokens, one exactly 768.
All inputs are finite; a program needn't handle non-finite values.
Results may differ from a plain program's by a relative error of at most 0.025.
Values may be sent and summed in bfloat16 or wider, within the bound.
A program may use at most 128 MiB of HBM per device.

v0:
```python
import jax
import jax.numpy as jnp
from jax import lax
from jax.sharding import PartitionSpec as P

TOK_DEV = 384
SEG_DEV = 2


soft_cap = 30.0
loss_scale = 1024.0


def body(hidden, head, teacher_logp, slot_blocks, segment_ids):
    voc_count = lax.axis_size("voc")
    tok_count = lax.axis_size("tok")
    tok_rows = hidden.shape[0]
    voc_cols = head.shape[1]
    blocks_each = slot_blocks.shape[0] // voc_count
    repeat = blocks_each // voc_count
    block_cols = voc_cols // blocks_each
    own_index = lax.axis_index("voc")
    slot_table = slot_blocks.reshape(voc_count, blocks_each)
    owners = slot_table // blocks_each
    send_order = jnp.argsort(owners, axis=1, stable=True)
    sorted_blocks = jnp.take_along_axis(slot_table, send_order, axis=1)
    tile_blocks = teacher_logp.reshape(tok_rows, blocks_each, block_cols)
    grouped = jnp.take(tile_blocks, send_order[own_index], axis=1).reshape(
        tok_rows, voc_count, repeat, block_cols
    )
    arrived = lax.all_to_all(grouped, "voc", split_axis=1, concat_axis=1, tiled=True)
    source_index = jnp.arange(voc_count, dtype=jnp.int32)
    source_rows = jnp.take(sorted_blocks, source_index, axis=0)
    arrived_ids = lax.dynamic_slice_in_dim(source_rows, own_index * repeat, repeat, 1)
    local_ids = arrived_ids.reshape(-1) - own_index * blocks_each
    inverse = jnp.argsort(local_ids)
    student_teacher = jnp.take(arrived.reshape(tok_rows, blocks_each, block_cols), inverse, axis=1)
    student_teacher = student_teacher.reshape(tok_rows, voc_cols)
    num_segments = SEG_DEV * tok_count
    onehot = (segment_ids[:, None] == jnp.arange(num_segments, dtype=jnp.int32)[None, :]).astype(
        jnp.float32
    )
    segment_count = lax.psum(jnp.sum(onehot, axis=0), "tok")
    seg_size = jnp.sum(onehot * segment_count[None, :], axis=1)
    token_weight = TOK_DEV / SEG_DEV / seg_size
    logits = jnp.dot(hidden, head, preferred_element_type=jnp.float32)
    capped = soft_cap * jnp.tanh(logits / soft_cap)
    teacher_prob = jnp.exp(student_teacher.astype(jnp.float32))
    local_mass = jnp.sum(teacher_prob, axis=1)
    shifted = jnp.exp(capped - soft_cap)
    student_total, teacher_mass = lax.psum((jnp.sum(shifted, axis=1), local_mass), "voc")
    grad_logits = (
        loss_scale
        * token_weight[:, None]
        * (shifted / student_total[:, None] * teacher_mass[:, None] - teacher_prob)
        * (1.0 - (capped / soft_cap) ** 2)
    ).astype(jnp.bfloat16)
    hidden_share = lax.psum_scatter(
        lax.dot_general(
            head, grad_logits, (((1,), (1,)), ((), ())), preferred_element_type=jnp.float32
        ).astype(jnp.bfloat16),
        "voc",
        scatter_dimension=0,
        tiled=True,
    ).astype(jnp.float32)
    d_hidden = hidden_share.T.astype(jnp.bfloat16)
    d_head = lax.psum_scatter(
        lax.dot_general(
            hidden, grad_logits, (((0,), (0,)), ((), ())), preferred_element_type=jnp.float32
        ).astype(jnp.bfloat16),
        "tok",
        scatter_dimension=0,
        tiled=True,
    ).astype(jnp.float32)
    return (d_hidden, d_head)


def solution(mesh):
    placed = (P("tok", None), P(None, "voc"), P("tok", "voc"), P(), P("tok"))
    return jax.shard_map(
        body,
        mesh=mesh,
        in_specs=placed,
        out_specs=(P("tok", "voc"), P("tok", "voc")),
        check_vma=False,
    )
```

profile of v0, /device:TPU:34, one launch (start us, length us, event | category | flops | bytes accessed | tf_op | source)
XLA Modules:
  0.0 360.8 jit_solution(11098188850133225704)
XLA Ops:
  11.1 1.3 sort.35
  12.4 1.6 reshape.49
  14.0 1.9 gather_fusion.2
  15.9 1.6 broadcast_select_fusion
  17.6 2.8 copy.41
  20.4 6.0 %all-to-all-start = ((bf16[384,8,2,125]{0,2,3,1:T(2,128)(2,1)}), bf16[384,8,2,125]{0,2,3,1:T(2,128)(2,1)}, u32[]{:S(2)}, u32[]{:S(2)}) async-start(bf16[384,8,2,125]{0,2,3,1:T(2,128)(2,1)} %copy.41), calls=%async_computation | async-start | bytes 3072000 | tf_op jit(solution)/shard_map/all_to_all | solution.py:31
  26.5 83.5 %psum.21 = f32[64]{0:T(128)S(1)} all-reduce(f32[64]{0:T(128)S(1)} %convert_reduce_fusion), channel_id=1, replica_groups=mesh['tok'=32,'voc'=8] {'tok'}, use_global_device_ids=true, to_apply=%region_1.2 | all-reduce | flops 64 | bytes 512 | tf_op jit(solution)/shard_map/psum | solution.py:43
  110.1 10.5 %fusion.2 = (f32[384]{0:T(512)S(1)}, f32[384,2000]{0,1:T(8,128)}) fusion(bf16[384,2304]{1,0:T(8,128)(2,1)S(1)} %copy-done, bf16[2304,2000]{0,1:T(8,128)(2,1)} %param.8), kind=kOutput, calls=%fused_computation.11 | convolution fusion | flops 3542015488 | bytes 14059008 | tf_op jit(solution)/shard_map/dot_general | solution.py:46
  120.6 3.7 %copy.42 = bf16[384,8,2,125]{3,0,2,1:T(8,128)(2,1)S(1)} copy(bf16[384,8,2,125]{0,2,3,1:T(2,128)(2,1)} %all-to-all-done) | data formatting | bytes 3072000 | tf_op jit(solution)/shard_map/all_to_all | solution.py:31
  124.3 1.9 gather_fusion.3
  126.2 3.8 %fusion.5 = (f32[384]{0:T(512)S(1)}, f32[384,16,125]{2,0,1:T(8,128)}) fusion(bf16[16,384,125]{2,1,0:T(8,128)(2,1)} %gather_fusion.3, pred[16]{0:T(512)(128)(4,1)S(1)} %get-tuple-element.25), kind=kLoop, calls=%fused_computation.39 | loop fusion | flops 2303616 | bytes 4609552 | tf_op jit(solution)/shard_map/reduce_sum | solution.py:49
  130.0 3.7 %copy.43 = f32[384,16,125]{0,2,1:T(8,128)} copy(f32[384,16,125]{2,0,1:T(8,128)} %get-tuple-element.22) | data formatting | bytes 6144000 | tf_op jit(solution)/shard_map/exp | solution.py:48
  133.7 3.3 exp.12
  137.0 14.9 %all-reduce = (f32[384]{0:T(512)S(1)}, f32[384]{0:T(512)S(1)}) all-reduce(f32[384]{0:T(512)S(1)} %get-tuple-element.21, f32[384]{0:T(512)S(1)} %get-tuple-element.23), channel_id=1, replica_groups=mesh['tok'=32,'voc'=8] {'voc'}, use_global_device_ids=true, to_apply=%region_8.10 | all-reduce | flops 768 | bytes 6144 | tf_op jit(solution)/shard_map/psum | solution.py:51
  151.9 4.0 %multiply_convert_fusion = bf16[384,2000]{0,1:T(8,128)(2,1)S(1)} fusion(f32[384,2000]{0,1:T(8,128)} %get-tuple-element.24, f32[384,2000]{0,1:T(8,128)} %exp.12, f32[384]{0:T(512)S(1)} %get-tuple-element.19, f32[384]{0:T(512)S(1)} %get-tuple-element.20, f32[384]{0:T(512)S(1)} %divide_multiply_fusion), kind=kLoop, calls=%fused_computation.9 | loop fusion | flops 7680000 | bytes 7684608 | tf_op jit(solution)/shard_map/convert_element_type | solution.py:57
  155.9 1.1 copy-done.1
  157.0 7.2 %fusion = bf16[2304,2000]{0,1:T(8,128)(2,1)} fusion(bf16[384,2000]{0,1:T(8,128)(2,1)S(1)} %multiply_convert_fusion, bf16[384,2304]{1,0:T(8,128)(2,1)S(1)} %copy-done), kind=kOutput, calls=%fused_computation.5 | convolution fusion | flops 3543552000 | bytes 12521472 | tf_op jit(solution)/shard_map/dot_general | solution.py:68
  164.2 12.8 %copy.48 = bf16[2304,2000]{1,0:T(8,128)(2,1)} copy(bf16[2304,2000]{0,1:T(8,128)(2,1)} %fusion) | data formatting | bytes 18432000
  177.0 8.0 %fusion.1 = bf16[2304,384]{0,1:T(8,128)(2,1)S(1)} fusion(bf16[384,2000]{0,1:T(8,128)(2,1)} %copy-done.1, bf16[2304,2000]{0,1:T(8,128)(2,1)} %param.8), kind=kOutput, calls=%fused_computation.7 | convolution fusion | flops 3539828736 | bytes 12521472 | tf_op jit(solution)/shard_map/dot_general | solution.py:59
  185.0 2.2 copy.46
  187.3 117.2 %reduce-scatter.9.cloned.1.call-done = bf16[72,2000]{1,0:T(8,128)(2,1)} async-done(((bf16[2304,2000]{1,0:T(8,128)(2,1)}), bf16[72,2000]{1,0:T(8,128)(2,1)}) %reduce-scatter.9.cloned.1.call-update) | async-done | bytes 288016
  304.5 1.3 copy.49
  305.8 1.0 copy.45
  306.8 47.2 %reduce-scatter.7.cloned.1.call-done = bf16[288,384]{1,0:T(8,128)(2,1)} async-done(((bf16[2304,384]{1,0:T(8,128)(2,1)}), bf16[288,384]{1,0:T(8,128)(2,1)}) %reduce-scatter.7.cloned.1.call-update) | async-done | bytes 221200
  (38 shorter events, 4.2 us)
Async XLA Ops:
  7.2 102.9 %copy-start = (bf16[384,2304]{1,0:T(8,128)(2,1)S(1)}, bf16[384,2304]{1,0:T(8,128)(2,1)}, u32[]{:S(2)}) copy-start(bf16[384,2304]{1,0:T(8,128)(2,1)} %param.7) | copy-start | bytes 5308420
  17.6 8.8 %copy-start.2 = (s32[384]{0:T(512)S(1)}, s32[384]{0:T(512)}, u32[]{:S(2)}) copy-start(s32[384]{0:T(512)} %param.11) | copy-start | bytes 4612
  20.4 100.2 %all-to-all-start = ((bf16[384,8,2,125]{0,2,3,1:T(2,128)(2,1)}), bf16[384,8,2,125]{0,2,3,1:T(2,128)(2,1)}, u32[]{:S(2)}, u32[]{:S(2)}) async-start(bf16[384,8,2,125]{0,2,3,1:T(2,128)(2,1)} %copy.41), calls=%async_computation | async-start | bytes 3072000 | tf_op jit(solution)/shard_map/all_to_all | solution.py:31
  26.4 278.1 %reduce-scatter.9.cloned.1.call-start = ((), (), s32[]{:S(2)}) async-start(), calls=%async_computation.4 | async-start | bytes 9732096
  155.9 1.2 copy-start.1
  177.0 177.0 %reduce-scatter.7.cloned.1.call-start = ((), (), s32[]{:S(2)}) async-start(), calls=%async_computation.3 | async-start | bytes 1990656
Sparse Core Ops, SparseCore 0:
  177.1 127.3 reduce-scatter.8
  307.8 46.0 reduce-scatter.6
where the time goes:
time: 364 us; the launch traced here: 361 us
  waiting for transfers between devices  164 us (45%)
  blocking collectives  98.4 us (27%)
  local copies, waits for them, and re-layouts  40.3 us (11%)
  matrix products  25.7 us (7%)
  between operations  14.2 us (4%)
  other arithmetic  11.8 us (3%)
  starting transfers between devices  6.05 us (2%)
    unnamed x4, waiting for transfers between devices  164 us
    psum x1, blocking collectives, body(): segment_count = lax.psum(jnp.sum(onehot, axis=0), 'tok')  83.5 us
    unnamed x10, local copies, waits for them, and re-layouts  18.4 us
    psum x1, blocking collectives, body(): lax.psum((jnp.sum(shifted, axis=1), local_mass), 'voc')  14.9 us
    dot_general x1, matrix products, body(): logits = jnp.dot(hidden, head, preferred_element_type=jnp.float32)  10.5 us
    dot_general x1, matrix products, body(): lax.dot_general(head, grad_logits, (((1,), (1,)), ((), ())), preferred_el...  7.97 us
  transfers between devices with their start and end apart: 3, of which 2 were waited for; matrix products, arithmetic and copies ran while one was open for 6% of the time, Pallas kernels for 0%

commit v1 on v0

v1 whole, which is shorter than its diff:
```python
import jax
import jax.numpy as jnp
from jax import lax
from jax.experimental import pallas as pl
from jax.experimental.pallas import tpu as pltpu
from jax.sharding import PartitionSpec as P

MESH = pl.DeviceIdType.MESH
F32 = jnp.float32
BF16 = jnp.bfloat16

NTOK = 32
NVOC = 8
T = 384
D = 2304
V = 2000
NBLK = 16
BC = 125
LAST = V - 15 * 128
R = D // NTOK
RY = 4 * R
RV = D // NVOC
SEGS = 64
SEG_WEIGHT = 192.0
CAP = 30.0
SCALE = 1024.0

LAG_C1 = 2
LAG_C2 = 3
LAG_C3 = 4
LAG_C4 = 5
TICKS = 8 + LAG_C4
TICK_H = 4


def dot(a, b):
    return jnp.dot(a, b, preferred_element_type=F32)


def dot_nt(a, b):
    return lax.dot_general(a, b, (((1,), (1,)), ((), ())), preferred_element_type=F32)


def kernel(
    slot, seg, hid_h, head_h, tea_h, dhid_o, dhead_o,
    tea_v, hid_v, head_v, headl, tblk, tsend, trec, idb, h32, hsend, ht, lnat,
    pblk, qblk, acc_t, acc_m, tots, arow, wrow, gc, gslot, gnat,
    yfar_s, yfar_r, ydir_s, ydir_r, yst_s, yst_r, ymid, yown,
    zfar_s, zfar_r, zdir_s, zdir_r, zst_s, zst_r, fin,
    xfar_s, xfar_r, xdir_s, xdir_r, xst_s, xst_r, xmid, xown, zl_s, zl_r,
    snd, blk, inv,
    lsem, id_ss, id_rs, t_ss, t_rs, ht_ss, ht_rs, tot_ss, tot_rs, g_ss, g_rs,
    yfar_ss, yfar_rs, ydir_ss, ydir_rs, yst_ss, yst_rs,
    zfar_ss, zfar_rs, zdir_ss, zdir_rs, zst_ss, zst_rs,
    xfar_ss, xfar_rs, xdir_ss, xdir_rs, xst_ss, xst_rs, zl_ss, zl_rs,
):
    t = lax.axis_index("tok")
    v = lax.axis_index("voc")
    c = lax.rem(t, 2)
    y = lax.rem(lax.div(t, 2), 4)
    zh = lax.div(t, 8)
    x = lax.div(v, 2)
    zl = lax.rem(v, 2)

    def at_y(step):
        return (zh * 8 + lax.rem(y + step + 4, 4) * 2 + c, v)

    def at_z(step):
        return (lax.rem(zh + step + 4, 4) * 8 + y * 2 + c, v)

    def at_x(step):
        return (t, lax.rem(x + step + 4, 4) * 2 + zl)

    sibling = (t + 1 - 2 * c, v)
    zl_peer = (t, v + 1 - 2 * zl)

    def at_v(step):
        return (t, lax.rem(v + step, NVOC))

    def at_t(step):
        return (lax.rem(t + step + NTOK, NTOK), v)

    def send(src, dst, ss, rs, device):
        return pltpu.make_async_remote_copy(
            src_ref=src, dst_ref=dst, send_sem=ss, recv_sem=rs, device_id=device, device_id_type=MESH
        )

    id_steps = (1, -1, 2, -2)

    barrier = pltpu.get_barrier_semaphore()
    partners = [sibling, at_y(1), at_y(-1), at_z(1), at_z(-1)]
    partners += [at_v(s) for s in range(1, NVOC)] + [at_t(s) for s in id_steps]
    for device in partners:
        pl.semaphore_signal(barrier, inc=1, device_id=device, device_id_type=MESH)

    tea_copy = pltpu.make_async_copy(tea_h, tea_v, lsem.at[0])
    hid_copy = pltpu.make_async_copy(hid_h, hid_v, lsem.at[1])
    head_copy = pltpu.make_async_copy(head_h, head_v, lsem.at[2])
    tea_copy.start()
    hid_copy.start()
    head_copy.start()

    @pl.loop(0, NVOC)
    def _(d):
        low = lax.rem(v + d, NVOC) * NBLK
        first = jnp.int32(0)
        last = jnp.int32(0)
        for j in range(NBLK):
            e = slot[v * NBLK + j]
            last = jnp.where((e >= low) & (e < low + NBLK), j, last)
            e = slot[v * NBLK + NBLK - 1 - j]
            first = jnp.where((e >= low) & (e < low + NBLK), NBLK - 1 - j, first)
        snd[2 * d] = first
        snd[2 * d + 1] = last

    @pl.loop(0, NVOC)
    def _(k):
        base = lax.rem(v + k, NVOC) * NBLK
        low = v * NBLK
        first = jnp.int32(0)
        last = jnp.int32(0)
        for j in range(NBLK):
            e = slot[base + j]
            last = jnp.where((e >= low) & (e < low + NBLK), e - low, last)
            e = slot[base + NBLK - 1 - j]
            first = jnp.where((e >= low) & (e < low + NBLK), e - low, first)
        blk[2 * k] = first
        blk[2 * k + 1] = last

    @pl.loop(0, NBLK)
    def _(b):
        place = jnp.int32(0)
        for s in range(NBLK):
            place = jnp.where(blk[s] == b, s, place)
        inv[b] = place

    idb[0] = jnp.broadcast_to(seg[...], (8, T))

    tea_copy.wait()

    @pl.loop(0, T // 64)
    def _(i):
        rows = pl.ds(pl.multiple_of(i * 64, 64), 64)
        lane = lax.broadcasted_iota(jnp.int32, (64, 128), 1)
        mass = jnp.zeros((64, 128), F32)
        before = None
        for b in range(NBLK):
            if b < 15:
                tile = tea_v[rows, b * 128 : b * 128 + 128].astype(F32)
                mass += jnp.exp(tile)
            else:
                tile = jnp.concatenate(
                    [tea_v[rows, 1920:V].astype(F32), jnp.zeros((64, 128 - LAST), F32)], axis=1
                )
                mass += jnp.where(lane < LAST, jnp.exp(tile), 0.0)
            block = tile
            if b > 0:
                block = pltpu.roll(jnp.where(lane >= 128 - 3 * b, before, tile), 3 * b, 1)
            tblk[b, rows, :] = block.astype(BF16)
            before = tile
        acc_m[rows, :] = mass

    for d in range(NVOC):
        for r in range(2):
            target = trec.at[0] if d == 0 else tsend.at[d]
            target[:, r * 128 : r * 128 + 128] = tblk[snd[2 * d + r]]

    def tea_send(d):
        return send(tsend.at[d], trec.at[NVOC - d], t_ss.at[d], t_rs.at[NVOC - d], at_v(d))

    def id_send(i):
        return send(idb.at[0], idb.at[i + 1], id_ss.at[i], id_rs.at[i], at_t(id_steps[i]))

    pl.semaphore_wait(barrier, len(partners))
    for i in range(4):
        id_send(i).start()
    for d in range(NVOC - 1, 4, -1):
        tea_send(d).start()

    hid_copy.wait()

    @pl.loop(0, D // 128)
    def _(j):
        off = pl.multiple_of(j * 128, 128)
        h32[pl.ds(off, 128), :] = hid_v[:, pl.ds(off, 128)].astype(F32).T

    def pack(core, yy):
        parts = []
        for z in range(4):
            parts.append(h32[pl.ds(pl.multiple_of((8 * z + 2 * yy + core) * R, 8), R), :])
        return jnp.concatenate(parts, axis=0).astype(BF16)

    @pl.loop(0, 4)
    def _(yy):
        hsend[yy] = pack(1 - c, yy)

    ht_send = send(hsend, ht.at[:, :, pl.ds(T, T)], ht_ss, ht_rs, sibling)
    ht_send.start()

    @pl.loop(0, 4)
    def _(yy):
        ht[yy, :, 0:T] = pack(c, yy)

    head_copy.wait()
    headl[...] = jnp.concatenate([head_v[:, 1920:V], jnp.zeros((D, 128 - LAST), BF16)], axis=1)

    @pl.loop(0, 7)
    def _(j):
        cols = pl.ds(pl.multiple_of(j * 256, 256), 256)
        lnat[:, cols] = dot(hid_v[...], head_v[:, cols])

    lnat[:, 1792:2048] = dot(
        hid_v[...], jnp.concatenate([head_v[:, 1792:1920], headl[...]], axis=1)
    )

    @pl.loop(0, T // 64)
    def _(i):
        rows = pl.ds(pl.multiple_of(i * 64, 64), 64)
        lane = lax.broadcasted_iota(jnp.int32, (64, 128), 1)
        total = jnp.zeros((64, 128), F32)
        for b in range(NBLK):
            logit = lnat[rows, b * 128 : b * 128 + 128]
            if b > 0:
                before = lnat[rows, b * 128 - 128 : b * 128]
                logit = pltpu.roll(jnp.where(lane >= 128 - 3 * b, before, logit), 3 * b, 1)
            th = jnp.tanh(logit * (1.0 / CAP))
            shifted = jnp.exp(CAP * th - CAP)
            slope = 1.0 - th * th
            total += jnp.where(lane < BC, shifted, 0.0)
            pblk[b, rows, :] = shifted * slope
            qblk[b, rows, :] = slope
        acc_t[rows, :] = total

    sub = lax.broadcasted_iota(jnp.int32, (8, T), 0)
    total_row = jnp.sum(acc_t[...].T, axis=0, keepdims=True)
    mass_row = jnp.sum(acc_m[...].T, axis=0, keepdims=True)
    tots[0] = jnp.where(sub == 0, total_row, mass_row)

    def tot_send(d):
        return send(tots.at[0], tots.at[NVOC - d], tot_ss.at[d], tot_rs.at[NVOC - d], at_v(d))

    for d in range(1, NVOC):
        tot_send(d).start()
    for d in range(4, 0, -1):
        tea_send(d).start()

    for i in range(4):
        id_send(i).wait_recv()
    segments = lax.broadcasted_iota(jnp.int32, (SEGS, T), 0)
    own_hit = segments == idb[0, 0:1, :]
    hits = own_hit.astype(F32)
    for i in range(1, 5):
        hits += (segments == idb[i, 0:1, :]).astype(F32)
    counts = jnp.sum(hits, axis=1, keepdims=True)
    seg_size = jnp.sum(jnp.where(own_hit, counts, 0.0), axis=0, keepdims=True)
    weight = (SCALE * SEG_WEIGHT) / seg_size
    wrow[...] = jnp.broadcast_to(weight, (128, T)).T

    for d in range(1, NVOC):
        tot_send(NVOC - d).wait_recv()
    sums = tots[0]
    for d in range(1, NVOC):
        sums += tots[d]
    ratio = weight * (sums[1:2, :] / sums[0:1, :])
    arow[...] = jnp.broadcast_to(ratio, (128, T)).T

    ht_send.wait_recv()

    def g_send(k):
        return send(
            gc.at[k, pl.ds(0, T), :], gc.at[k, pl.ds(T, T), :], g_ss.at[k], g_rs.at[k], sibling
        )

    def yfar(k, r):
        return send(yfar_s.at[k, r], yfar_r.at[k, r], yfar_ss.at[k, r], yfar_rs.at[k, r], at_y(1 - 2 * r))

    def ydir(k, r):
        return send(ydir_s.at[k, r], ydir_r.at[k, r], ydir_ss.at[k, r], ydir_rs.at[k, r], at_y(2 * r - 1))

    def yst(k, r):
        return send(yst_s.at[k, r], yst_r.at[k, r], yst_ss.at[k, r], yst_rs.at[k, r], at_y(1 - 2 * r))

    def zway(k):
        return 1 - 2 * lax.rem(k, 2)

    def zfar(k):
        return send(zfar_s.at[k], zfar_r.at[k], zfar_ss.at[k], zfar_rs.at[k], at_z(zway(k)))

    def zdir(k):
        return send(zdir_s.at[k], zdir_r.at[k], zdir_ss.at[k], zdir_rs.at[k], at_z(-zway(k)))

    def zst(k):
        return send(zst_s.at[k], zst_r.at[k], zst_ss.at[k], zst_rs.at[k], at_z(zway(k)))

    def grads(k):
        @pl.when(k > 0)
        def _():
            tea_send(NVOC - k).wait_recv()

        @pl.loop(0, T // 128)
        def _(i):
            rows = pl.ds(pl.multiple_of(i * 128, 128), 128)
            for r in range(2):
                b = blk[2 * k + r]
                prob = jnp.exp(trec[k, rows, r * 128 : r * 128 + 128].astype(F32))
                grad = arow[rows, :] * pblk[b, rows, :] - wrow[rows, :] * prob * qblk[b, rows, :]
                grad = grad.astype(BF16)
                gc[k, rows, r * 128 : r * 128 + 128] = grad
                gslot[2 * k + r, rows, :] = grad

        g_send(k).start()

    def mm(k):
        g_send(k).wait_recv()
        far = dot(ht[lax.rem(y + 2, 4)], gc[k])
        for r in range(2):
            yfar_s[k, r] = far[:, r * 128 : r * 128 + 128].astype(BF16)
            yfar(k, r).start()
        part = dot(ht[lax.rem(y + 1, 4)], gc[k])
        ydir_s[k, 1] = part[:, 128:].astype(BF16)
        ydir(k, 1).start()
        ymid[k, 0] = part[:, :128]
        part = dot(ht[lax.rem(y + 3, 4)], gc[k])
        ydir_s[k, 0] = part[:, :128].astype(BF16)
        ydir(k, 0).start()
        ymid[k, 1] = part[:, 128:]
        yown[k] = dot(ht[y], gc[k])

    def c1(k):
        for r in range(2):
            yfar(k, r).wait_recv()
            yst_s[k, r] = (ymid[k, r] + yfar_r[k, r].astype(F32)).astype(BF16)
            yst(k, r).start()

    def zrows(k, step):
        rows = pl.ds(pl.multiple_of(lax.rem(zh + step + 4, 4) * R, 8), R)
        return jnp.concatenate([yown[k, rows, 0:128], yown[k, rows, 128:256]], axis=0)

    def c2(k):
        for r in range(2):
            ydir(k, r).wait_recv()
            yst(k, r).wait_recv()
            lanes = slice(r * 128, r * 128 + 128)
            yown[k, :, lanes] += ydir_r[k, r].astype(F32) + yst_r[k, r].astype(F32)
        zfar_s[k] = zrows(k, 2).astype(BF16)
        zfar(k).start()
        zdir_s[k] = zrows(k, -zway(k)).astype(BF16)
        zdir(k).start()

    def c3(k):
        zfar(k).wait_recv()
        zst_s[k] = (zrows(k, zway(k)) + zfar_r[k].astype(F32)).astype(BF16)
        zst(k).start()

    def c4(k):
        zdir(k).wait_recv()
        zst(k).wait_recv()
        done = zrows(k, 0) + (zdir_r[k].astype(F32) + zst_r[k].astype(F32))
        fin[2 * k] = done[0:R]
        fin[2 * k + 1] = done[R : 2 * R]

    def xfar(h):
        return send(xfar_s.at[h], xfar_r.at[h], xfar_ss.at[h], xfar_rs.at[h], at_x(1 - 2 * h))

    def xdir(h):
        return send(xdir_s.at[h], xdir_r.at[h], xdir_ss.at[h], xdir_rs.at[h], at_x(2 * h - 1))

    def xst(h):
        return send(xst_s.at[h], xst_r.at[h], xst_ss.at[h], xst_rs.at[h], at_x(1 - 2 * h))

    zlx = send(zl_s, zl_r, zl_ss, zl_rs, zl_peer)

    def natural():
        @pl.loop(0, T // 64)
        def _(i):
            rows = pl.ds(pl.multiple_of(i * 64, 64), 64)
            lane = lax.broadcasted_iota(jnp.int32, (64, 128), 1)

            def rolled(b):
                s = inv[b]
                block = gslot[s, rows, :].astype(F32)
                return pltpu.roll(block, 128 - 3 * b, 1) if b else block

            here = rolled(0)
            for q in range(NBLK):
                after = rolled(q + 1) if q < 15 else jnp.zeros((64, 128), F32)
                gnat[rows, q * 128 : q * 128 + 128] = jnp.where(
                    lane < BC - 3 * q, here, after
                ).astype(BF16)
                here = after

    def part_h(step, h):
        rows = pl.ds(pl.multiple_of((lax.rem(x + step, 4) * 2 + h) * RV, 16), RV)
        return dot_nt(head_v[rows, 0:1920], gnat[:, 0:1920]) + dot_nt(headl[rows, :], gnat[:, 1920:2048])

    def h0():
        natural()
        for h in range(2):
            xfar_s[h] = part_h(2, h).astype(BF16)
            xfar(h).start()
        xdir_s[1] = part_h(1, 1).astype(BF16)
        xdir(1).start()
        xdir_s[0] = part_h(3, 0).astype(BF16)
        xdir(0).start()

    def h1():
        xmid[0] = part_h(1, 0)
        xmid[1] = part_h(3, 1)
        for h in range(2):
            xfar(h).wait_recv()
            xst_s[h] = (xmid[h] + xfar_r[h].astype(F32)).astype(BF16)
            xst(h).start()
        for h in range(2):
            xown[h] = part_h(0, h)

    def h2():
        for h in range(2):
            xdir(h).wait_recv()
            xst(h).wait_recv()
            xown[h] += xdir_r[h].astype(F32) + xst_r[h].astype(F32)
        zl_s[...] = xown[1 - zl].astype(BF16)
        zlx.start()

    def h3():
        zlx.wait_recv()
        full = xown[zl] + zl_r[...].astype(F32)
        dhid_o[...] = full.T.astype(BF16)

    @pl.loop(0, TICKS)
    def _(n):
        def stage(f, lag):
            @pl.when((n >= lag) & (n < lag + NVOC))
            def _():
                f(n - lag)

        stage(c1, LAG_C1)

        @pl.when(n < 4)
        def _():
            grads(2 * n)
            grads(2 * n + 1)

        stage(mm, 0)
        stage(c2, LAG_C2)
        stage(c3, LAG_C3)
        stage(c4, LAG_C4)
        pl.when(n == TICK_H)(h0)
        pl.when(n == TICK_H + 1)(h1)
        pl.when(n == TICK_H + 4)(h2)
        pl.when(n == TICK_H + 6)(h3)

    lane = lax.broadcasted_iota(jnp.int32, (R, 128), 1)

    def rolled_out(b):
        block = fin[inv[b]]
        return pltpu.roll(block, 128 - 3 * b, 1) if b else block

    here = rolled_out(0)
    for q in range(NBLK):
        after = rolled_out(q + 1) if q < 15 else here
        tile = jnp.where(lane < BC - 3 * q, here, after)
        if q < 15:
            dhead_o[:, q * 128 : q * 128 + 128] = tile
        else:
            dhead_o[:, 1920:V] = tile[:, 0:LAST]
        here = after

    for i in range(4):
        id_send(i).wait_send()
    for d in range(1, NVOC):
        tea_send(d).wait_send()
        tot_send(d).wait_send()
    ht_send.wait_send()

    @pl.loop(0, NVOC)
    def _(k):
        g_send(k).wait_send()
        for r in range(2):
            yfar(k, r).wait_send()
            ydir(k, r).wait_send()
            yst(k, r).wait_send()
        zfar(k).wait_send()
        zdir(k).wait_send()
        zst(k).wait_send()

    for h in range(2):
        xfar(h).wait_send()
        xdir(h).wait_send()
        xst(h).wait_send()
    zlx.wait_send()


def body(hidden, head, teacher_logp, slot_blocks, segment_ids):
    vm = pltpu.VMEM
    dma = pltpu.SemaphoreType.DMA
    chunk = (NVOC, 2)
    scratch = [
        vm((T, V), BF16),
        vm((T, D), BF16),
        vm((D, V), BF16),
        vm((D, 128), BF16),
        vm((NBLK, T, 128), BF16),
        vm((NVOC, T, 256), BF16),
        vm((NVOC, T, 256), BF16),
        vm((5, 8, T), jnp.int32),
        vm((D, T), F32),
        vm((4, RY, T), BF16),
        vm((4, RY, 2 * T), BF16),
        vm((T, 2048), F32),
        vm((NBLK, T, 128), F32),
        vm((NBLK, T, 128), F32),
        vm((T, 128), F32),
        vm((T, 128), F32),
        vm((NVOC, 8, T), F32),
        vm((T, 128), F32),
        vm((T, 128), F32),
        vm((NVOC, 2 * T, 256), BF16),
        vm((NBLK, T, 128), BF16),
        vm((T, 2048), BF16),
    ]
    scratch += [vm(chunk + (RY, 128), BF16)] * 6
    scratch += [vm(chunk + (RY, 128), F32), vm((NVOC, RY, 256), F32)]
    scratch += [vm((NVOC, 2 * R, 128), BF16)] * 6
    scratch += [vm((NBLK, R, 128), F32)]
    scratch += [vm((2, RV, T), BF16)] * 6
    scratch += [vm((2, RV, T), F32)] * 2
    scratch += [vm((RV, T), BF16)] * 2
    scratch += [pltpu.SMEM((NBLK,), jnp.int32)] * 3
    scratch += [dma((3,)), dma((4,)), dma((4,)), dma((NVOC,)), dma((NVOC,)), dma(()), dma(())]
    scratch += [dma((NVOC,))] * 4
    scratch += [dma(chunk)] * 6 + [dma((NVOC,))] * 6 + [dma((2,))] * 6 + [dma(())] * 2
    anywhere = pl.BlockSpec(memory_space=pl.ANY)
    in_vmem = pl.BlockSpec(memory_space=pltpu.VMEM)
    return pl.pallas_call(
        kernel,
        out_shape=(
            jax.ShapeDtypeStruct((T, RV), BF16),
            jax.ShapeDtypeStruct((R, V), F32),
        ),
        in_specs=[pl.BlockSpec(memory_space=pltpu.SMEM), in_vmem, anywhere, anywhere, anywhere],
        out_specs=(in_vmem, in_vmem),
        scratch_shapes=scratch,
        compiler_params=pltpu.CompilerParams(
            collective_id=0, has_side_effects=True, vmem_limit_bytes=63 * 2**20
        ),
    )(slot_blocks, segment_ids.reshape(1, T), hidden, head, teacher_logp)


def solution(mesh):
    placed = (P("tok", None), P(None, "voc"), P("tok", "voc"), P(), P("tok"))
    return jax.shard_map(
        body,
        mesh=mesh,
        in_specs=placed,
        out_specs=(P("tok", "voc"), P("tok", "voc")),
        check_vma=False,
    )
```

time: 364 us -> 113 us (0.31)
  the two profiles are of different devices: /device:TPU:34 before, /device:TPU:1 now
where the time goes in v1:
time: 113 us; the launch traced here: 112 us
  Pallas kernels  91.4 us (81%)
  local copies, waits for them, and re-layouts  20.3 us (18%)
    pallas_call x1, Pallas kernels, body(): pl.pallas_call(kernel, out_shape=(jax.ShapeDtypeStruct((T, RV), BF16), ja...  91.4 us
    unnamed x3, local copies, waits for them, and re-layouts  17.3 us

profile of v1, /device:TPU:1, one launch (start us, length us, event | category | flops | bytes accessed | tf_op | source)
XLA Modules:
  0.0 112.3 jit_solution(15746951786154765118)
XLA Ops:
  0.6 1.2 %reshape.7.seg = s32[1,384]{1,0:T(1,128)} reshape(s32[384]{0:T(512)} %param.9) | data formatting | bytes 3072 | tf_op jit(solution)/shard_map/reshape | solution.py:546
  1.9 2.6 %copy.8.tea_h = bf16[384,2000]{1,0:T(8,128)(2,1)} copy(bf16[384,2000]{0,1:T(8,128)(2,1)} %param.7) | data formatting | bytes 3072000 | tf_op args[2]
  4.5 12.8 %copy.7.head_h = bf16[2304,2000]{1,0:T(8,128)(2,1)} copy(bf16[2304,2000]{0,1:T(8,128)(2,1)} %param.6) | data formatting | bytes 18432000 | tf_op args[1]
  17.2 91.4 %shard_map.68 = (bf16[384,288]{1,0:T(8,128)(2,1)}, f32[72,2000]{1,0:T(8,128)}) custom-call(s32[128]{0:T(128)} %slot.1, s32[1,384]{1,0:T(1,128)} %reshape.7.seg, bf16[384,2304]{1,0:T(8,128)(2,1)} %hid_h.1, bf16[2304,2000]{1,0:T(8,128)(2,1)} %copy.7.head_h, bf16[384,2000]{1,0:T(8,128)(2,1)} %copy.8.tea_h), custom_call_target="tpu_custom_call" | custom-call | tf_op jit(solution)/shard_map/pallas_call | solution.py:534
  108.6 1.8 %copy.9 = bf16[384,288]{0,1:T(8,128)(2,1)} copy(bf16[384,288]{1,0:T(8,128)(2,1)} %get-tuple-element.2) | data formatting | bytes 442368 | tf_op jit(solution)/shard_map/pallas_call | solution.py:534
  110.4 1.9 %copy.11 = f32[72,2000]{1,0:T(8,128)} copy(f32[72,2000]{1,0:T(8,128)} %get-tuple-element.7) | data formatting | bytes 1152000

commit v2 on v1

--- a/solution.py
+++ b/solution.py
@@ -14,6 +14,7 @@
 T = 384
 D = 2304
 V = 2000
+VP = 2048
 NBLK = 16
 BC = 125
 LAST = V - 15 * 128
@@ -25,6 +26,8 @@
 CAP = 30.0
 SCALE = 1024.0
 
+ORDER = (0, 1, 2, 7, 6, 3, 4, 5)
+AHEAD = 8
 LAG_C1 = 2
 LAG_C2 = 3
 LAG_C3 = 4
@@ -43,13 +46,13 @@
 
 def kernel(
     slot, seg, hid_h, head_h, tea_h, dhid_o, dhead_o,
-    tea_v, hid_v, head_v, headl, tblk, tsend, trec, idb, h32, hsend, ht, lnat,
-    pblk, qblk, acc_t, acc_m, tots, arow, wrow, gc, gslot, gnat,
+    tea_v, hid_v, head_v, tea32, nat32, tblk, tsend, trec, idb, h32, htn, hsend, ht,
+    pblk, qblk, tots, arow, wrow, gc, gslot, gnat,
     yfar_s, yfar_r, ydir_s, ydir_r, yst_s, yst_r, ymid, yown,
     zfar_s, zfar_r, zdir_s, zdir_r, zst_s, zst_r, fin,
     xfar_s, xfar_r, xdir_s, xdir_r, xst_s, xst_r, xmid, xown, zl_s, zl_r,
     snd, blk, inv,
-    lsem, id_ss, id_rs, t_ss, t_rs, ht_ss, ht_rs, tot_ss, tot_rs, g_ss, g_rs,
+    lsem, hd_sem, id_ss, id_rs, t_ss, t_rs, ht_ss, ht_rs, tot_ss, tot_rs, g_ss, g_rs,
     yfar_ss, yfar_rs, ydir_ss, ydir_rs, yst_ss, yst_rs,
     zfar_ss, zfar_rs, zdir_ss, zdir_rs, zst_ss, zst_rs,
     xfar_ss, xfar_rs, xdir_ss, xdir_rs, xst_ss, xst_rs, zl_ss, zl_rs,
@@ -93,16 +96,108 @@
     for device in partners:
         pl.semaphore_signal(barrier, inc=1, device_id=device, device_id_type=MESH)
 
-    tea_copy = pltpu.make_async_copy(tea_h, tea_v, lsem.at[0])
+    tea_copy = pltpu.make_async_copy(tea_h, tea_v.at[pl.ds(0, V)], lsem.at[0])
     hid_copy = pltpu.make_async_copy(hid_h, hid_v, lsem.at[1])
-    head_copy = pltpu.make_async_copy(head_h, head_v, lsem.at[2])
+
+    def head_copy(p):
+        rows = pl.ds(p * 512, min(512, V - p * 512))
+        return pltpu.make_async_copy(head_h.at[rows], head_v.at[rows], hd_sem.at[p])
+
     tea_copy.start()
     hid_copy.start()
-    head_copy.start()
+
+    idb[0] = jnp.broadcast_to(seg[...].reshape(1, T), (8, T))
+
+    tea_v[V:VP, :] = jnp.zeros((VP - V, T), BF16)
+    head_v[V:VP, :] = jnp.zeros((VP - V, D), BF16)
+    tea_copy.wait()
+    head_copy(0).start()
+    head_copy(1).start()
+
+    def fold(values):
+        return jnp.sum(values.reshape(values.shape[0] // 8, 8, T), axis=0)
+
+    def tea_step(i, mass):
+        rows = pl.ds(pl.multiple_of(i * 80, 80), 80)
+        tile = tea_v[rows, :].astype(F32)
+        tea32[rows, :] = tile
+        return mass + fold(jnp.exp(tile))
+
+    mass_part = lax.fori_loop(0, V // 80, tea_step, jnp.zeros((8, T), F32))
+    tea32[V:VP, :] = jnp.zeros((VP - V, T), F32)
+
+    hid_copy.wait()
+
+    @pl.loop(0, D // 128)
+    def _(j):
+        off = pl.multiple_of(j * 128, 128)
+        turned = hid_v[:, pl.ds(off, 128)].astype(F32).T
+        h32[pl.ds(off, 128), :] = turned
+        htn[pl.ds(off, 128), :] = turned.astype(BF16)
+
+    total_part = jnp.zeros((8, T), F32)
+    valid = lax.broadcasted_iota(jnp.int32, (128, T), 0) < BC
+    for b in range(NBLK):
+        if b % 4 == 0:
+            head_copy(b // 4).wait()
+            if b < 8:
+                head_copy(b // 4 + 2).start()
+        nat32[b * 128 : b * 128 + 128, :] = dot(head_v[b * 128 : b * 128 + 128, :], htn[...])
+        th = jnp.tanh(nat32[b * BC : b * BC + 128, :] * (1.0 / CAP))
+        shifted = jnp.exp(CAP * th - CAP)
+        slope = 1.0 - th * th
+        pblk[b] = shifted * slope
+        qblk[b] = slope
+        total_part += fold(jnp.where(valid, shifted, 0.0))
+
+    sub = lax.broadcasted_iota(jnp.int32, (8, T), 0)
+    total_row = jnp.sum(total_part, axis=0, keepdims=True)
+    mass_row = jnp.sum(mass_part, axis=0, keepdims=True)
+    tots[0] = jnp.where(sub == 0, total_row, mass_row)
+
+    def tot_send(d):
+        return send(tots.at[0], tots.at[NVOC - d], tot_ss.at[d], tot_rs.at[NVOC - d], at_v(d))
+
+    pl.semaphore_wait(barrier, len(partners))
+    for d in range(1, NVOC):
+        tot_send(d).start()
+
+    def tea_send(k):
+        back = NVOC - (ORDER[k] if isinstance(k, int) else offset(k))
+        return send(tsend.at[k], trec.at[k], t_ss.at[k], t_rs.at[k], at_v(back))
+
+    def id_send(i):
+        return send(idb.at[0], idb.at[i + 1], id_ss.at[i], id_rs.at[i], at_t(id_steps[i]))
+
+    for i in range(4):
+        id_send(i).start()
+
+    def pack(core, yy):
+        parts = []
+        for z in range(4):
+            parts.append(h32[pl.ds(pl.multiple_of((8 * z + 2 * yy + core) * R, 8), R), :])
+        return jnp.concatenate(parts, axis=0).astype(BF16)
+
+    @pl.loop(0, 4)
+    def _(yy):
+        hsend[yy] = pack(1 - c, yy)
+
+    ht_send = send(hsend, ht.at[:, :, pl.ds(T, T)], ht_ss, ht_rs, sibling)
+    ht_send.start()
+
+    @pl.loop(0, 4)
+    def _(yy):
+        ht[yy, :, 0:T] = pack(c, yy)
+
+    def offset(k):
+        out = jnp.int32(0)
+        for i in range(1, NVOC):
+            out = jnp.where(k == i, ORDER[i], out)
+        return out
 
     @pl.loop(0, NVOC)
     def _(d):
-        low = lax.rem(v + d, NVOC) * NBLK
+        low = lax.rem(v + NVOC - offset(d), NVOC) * NBLK
         first = jnp.int32(0)
         last = jnp.int32(0)
         for j in range(NBLK):
@@ -113,9 +208,20 @@
         snd[2 * d] = first
         snd[2 * d + 1] = last
 
+    for b in range(NBLK):
+        tblk[b] = tea32[b * BC : b * BC + 128, :].astype(BF16)
+
+    for d in range(NVOC):
+        for r in range(2):
+            target = trec.at[0] if d == 0 else tsend.at[d]
+            target[r * 128 : r * 128 + 128, :] = tblk[snd[2 * d + r]]
+
+    for k in range(1, AHEAD):
+        tea_send(k).start()
+
     @pl.loop(0, NVOC)
     def _(k):
-        base = lax.rem(v + k, NVOC) * NBLK
+        base = lax.rem(v + offset(k), NVOC) * NBLK
         low = v * NBLK
         first = jnp.int32(0)
         last = jnp.int32(0)
@@ -134,116 +240,6 @@
             place = jnp.where(blk[s] == b, s, place)
         inv[b] = place
 
-    idb[0] = jnp.broadcast_to(seg[...], (8, T))
-
-    tea_copy.wait()
-
-    @pl.loop(0, T // 64)
-    def _(i):
-        rows = pl.ds(pl.multiple_of(i * 64, 64), 64)
-        lane = lax.broadcasted_iota(jnp.int32, (64, 128), 1)
-        mass = jnp.zeros((64, 128), F32)
-        before = None
-        for b in range(NBLK):
-            if b < 15:
-                tile = tea_v[rows, b * 128 : b * 128 + 128].astype(F32)
-                mass += jnp.exp(tile)
-            else:
-                tile = jnp.concatenate(
-                    [tea_v[rows, 1920:V].astype(F32), jnp.zeros((64, 128 - LAST), F32)], axis=1
-                )
-                mass += jnp.where(lane < LAST, jnp.exp(tile), 0.0)
-            block = tile
-            if b > 0:
-                block = pltpu.roll(jnp.where(lane >= 128 - 3 * b, before, tile), 3 * b, 1)
-            tblk[b, rows, :] = block.astype(BF16)
-            before = tile
-        acc_m[rows, :] = mass
-
-    for d in range(NVOC):
-        for r in range(2):
-            target = trec.at[0] if d == 0 else tsend.at[d]
-            target[:, r * 128 : r * 128 + 128] = tblk[snd[2 * d + r]]
-
-    def tea_send(d):
-        return send(tsend.at[d], trec.at[NVOC - d], t_ss.at[d], t_rs.at[NVOC - d], at_v(d))
-
-    def id_send(i):
-        return send(idb.at[0], idb.at[i + 1], id_ss.at[i], id_rs.at[i], at_t(id_steps[i]))
-
-    pl.semaphore_wait(barrier, len(partners))
-    for i in range(4):
-        id_send(i).start()
-    for d in range(NVOC - 1, 4, -1):
-        tea_send(d).start()
-
-    hid_copy.wait()
-
-    @pl.loop(0, D // 128)
-    def _(j):
-        off = pl.multiple_of(j * 128, 128)
-        h32[pl.ds(off, 128), :] = hid_v[:, pl.ds(off, 128)].astype(F32).T
-
-    def pack(core, yy):
-        parts = []
-        for z in range(4):
-            parts.append(h32[pl.ds(pl.multiple_of((8 * z + 2 * yy + core) * R, 8), R), :])
-        return jnp.concatenate(parts, axis=0).astype(BF16)
-
-    @pl.loop(0, 4)
-    def _(yy):
-        hsend[yy] = pack(1 - c, yy)
-
-    ht_send = send(hsend, ht.at[:, :, pl.ds(T, T)], ht_ss, ht_rs, sibling)
-    ht_send.start()
-
-    @pl.loop(0, 4)
-    def _(yy):
-        ht[yy, :, 0:T] = pack(c, yy)
-
-    head_copy.wait()
-    headl[...] = jnp.concatenate([head_v[:, 1920:V], jnp.zeros((D, 128 - LAST), BF16)], axis=1)
-
-    @pl.loop(0, 7)
-    def _(j):
-        cols = pl.ds(pl.multiple_of(j * 256, 256), 256)
-        lnat[:, cols] = dot(hid_v[...], head_v[:, cols])
-
-    lnat[:, 1792:2048] = dot(
-        hid_v[...], jnp.concatenate([head_v[:, 1792:1920], headl[...]], axis=1)
-    )
-
-    @pl.loop(0, T // 64)
-    def _(i):
-        rows = pl.ds(pl.multiple_of(i * 64, 64), 64)
-        lane = lax.broadcasted_iota(jnp.int32, (64, 128), 1)
-        total = jnp.zeros((64, 128), F32)
-        for b in range(NBLK):
-            logit = lnat[rows, b * 128 : b * 128 + 128]
-            if b > 0:
-                before = lnat[rows, b * 128 - 128 : b * 128]
-                logit = pltpu.roll(jnp.where(lane >= 128 - 3 * b, before, logit), 3 * b, 1)
-            th = jnp.tanh(logit * (1.0 / CAP))
-            shifted = jnp.exp(CAP * th - CAP)
-            slope = 1.0 - th * th
-            total += jnp.where(lane < BC, shifted, 0.0)
-            pblk[b, rows, :] = shifted * slope
-            qblk[b, rows, :] = slope
-        acc_t[rows, :] = total
-
-    sub = lax.broadcasted_iota(jnp.int32, (8, T), 0)
-    total_row = jnp.sum(acc_t[...].T, axis=0, keepdims=True)
-    mass_row = jnp.sum(acc_m[...].T, axis=0, keepdims=True)
-    tots[0] = jnp.where(sub == 0, total_row, mass_row)
-
-    def tot_send(d):
-        return send(tots.at[0], tots.at[NVOC - d], tot_ss.at[d], tot_rs.at[NVOC - d], at_v(d))
-
-    for d in range(1, NVOC):
-        tot_send(d).start()
-    for d in range(4, 0, -1):
-        tea_send(d).start()
-
     for i in range(4):
         id_send(i).wait_recv()
     segments = lax.broadcasted_iota(jnp.int32, (SEGS, T), 0)
@@ -254,7 +250,7 @@
     counts = jnp.sum(hits, axis=1, keepdims=True)
     seg_size = jnp.sum(jnp.where(own_hit, counts, 0.0), axis=0, keepdims=True)
     weight = (SCALE * SEG_WEIGHT) / seg_size
-    wrow[...] = jnp.broadcast_to(weight, (128, T)).T
+    wrow[...] = jnp.broadcast_to(weight, (8, T))
 
     for d in range(1, NVOC):
         tot_send(NVOC - d).wait_recv()
@@ -262,8 +258,10 @@
     for d in range(1, NVOC):
         sums += tots[d]
     ratio = weight * (sums[1:2, :] / sums[0:1, :])
-    arow[...] = jnp.broadcast_to(ratio, (128, T)).T
-
+    arow[...] = jnp.broadcast_to(ratio, (8, T))
+
+    for k in range(AHEAD, NVOC):
+        tea_send(k).start()
     ht_send.wait_recv()
 
     def g_send(k):
@@ -295,18 +293,15 @@
     def grads(k):
         @pl.when(k > 0)
         def _():
-            tea_send(NVOC - k).wait_recv()
-
-        @pl.loop(0, T // 128)
-        def _(i):
-            rows = pl.ds(pl.multiple_of(i * 128, 128), 128)
-            for r in range(2):
-                b = blk[2 * k + r]
-                prob = jnp.exp(trec[k, rows, r * 128 : r * 128 + 128].astype(F32))
-                grad = arow[rows, :] * pblk[b, rows, :] - wrow[rows, :] * prob * qblk[b, rows, :]
-                grad = grad.astype(BF16)
-                gc[k, rows, r * 128 : r * 128 + 128] = grad
-                gslot[2 * k + r, rows, :] = grad
+            tea_send(k).wait_recv()
+
+        for r in range(2):
+            b = blk[2 * k + r]
+            prob = jnp.exp(trec[k, r * 128 : r * 128 + 128, :].astype(F32))
+            grad = arow[0:1, :] * pblk[b] - wrow[0:1, :] * (prob * qblk[b])
+            grad = grad.T.astype(BF16)
+            gc[k, 0:T, r * 128 : r * 128 + 128] = grad
+            gslot[2 * k + r] = grad
 
         g_send(k).start()
 
@@ -391,10 +386,20 @@
 
     def part_h(step, h):
         rows = pl.ds(pl.multiple_of((lax.rem(x + step, 4) * 2 + h) * RV, 16), RV)
-        return dot_nt(head_v[rows, 0:1920], gnat[:, 0:1920]) + dot_nt(headl[rows, :], gnat[:, 1920:2048])
+        return h32[rows, :]
+
+    def hm(low, high):
+        @pl.loop(low, high)
+        def _(j):
+            cols = pl.ds(pl.multiple_of(j * 256, 256), 256)
+            h32[cols, :] = dot(gnat[...], head_v[:, cols]).T
+
+    def ha():
+        natural()
+        hm(0, 3)
 
     def h0():
-        natural()
+        hm(3, 9)
         for h in range(2):
             xfar_s[h] = part_h(2, h).astype(BF16)
             xfar(h).start()
@@ -424,7 +429,7 @@
     def h3():
         zlx.wait_recv()
         full = xown[zl] + zl_r[...].astype(F32)
-        dhid_o[...] = full.T.astype(BF16)
+        dhid_o[...] = full.astype(BF16)
 
     @pl.loop(0, TICKS)
     def _(n):
@@ -435,19 +440,32 @@
 
         stage(c1, LAG_C1)
 
-        @pl.when(n < 4)
+        @pl.when(n == 0)
+        def _():
+            grads(0)
+
+        stage(mm, 0)
+
+        @pl.when(n < 2)
+        def _():
+            grads(n + 1)
+
+        @pl.when((n >= 2) & (n < 5))
+        def _():
+            grads(2 * n - 1)
+
+        @pl.when((n >= 2) & (n < 4))
         def _():
             grads(2 * n)
-            grads(2 * n + 1)
-
-        stage(mm, 0)
+
         stage(c2, LAG_C2)
         stage(c3, LAG_C3)
         stage(c4, LAG_C4)
-        pl.when(n == TICK_H)(h0)
-        pl.when(n == TICK_H + 1)(h1)
-        pl.when(n == TICK_H + 4)(h2)
-        pl.when(n == TICK_H + 6)(h3)
+        pl.when(n == TICK_H)(ha)
+        pl.when(n == TICK_H + 1)(h0)
+        pl.when(n == TICK_H + 3)(h1)
+        pl.when(n == TICK_H + 6)(h2)
+        pl.when(n == TICK_H + 8)(h3)
 
     lane = lax.broadcasted_iota(jnp.int32, (R, 128), 1)
 
@@ -495,28 +513,27 @@
     dma = pltpu.SemaphoreType.DMA
     chunk = (NVOC, 2)
     scratch = [
-        vm((T, V), BF16),
+        vm((VP, T), BF16),
         vm((T, D), BF16),
-        vm((D, V), BF16),
-        vm((D, 128), BF16),
-        vm((NBLK, T, 128), BF16),
-        vm((NVOC, T, 256), BF16),
-        vm((NVOC, T, 256), BF16),
+        vm((VP, D), BF16),
+        vm((VP, T), F32),
+        vm((VP, T), F32),
+        vm((NBLK, 128, T), BF16),
+        vm((NVOC, 256, T), BF16),
+        vm((NVOC, 256, T), BF16),
         vm((5, 8, T), jnp.int32),
         vm((D, T), F32),
+        vm((D, T), BF16),
         vm((4, RY, T), BF16),
         vm((4, RY, 2 * T), BF16),
-        vm((T, 2048), F32),
-        vm((NBLK, T, 128), F32),
-        vm((NBLK, T, 128), F32),
-        vm((T, 128), F32),
-        vm((T, 128), F32),
+        vm((NBLK, 128, T), F32),
+        vm((NBLK, 128, T), F32),
         vm((NVOC, 8, T), F32),
-        vm((T, 128), F32),
-        vm((T, 128), F32),
+        vm((8, T), F32),
+        vm((8, T), F32),
         vm((NVOC, 2 * T, 256), BF16),
         vm((NBLK, T, 128), BF16),
-        vm((T, 2048), BF16),
+        vm((T, VP), BF16),
     ]
     scratch += [vm(chunk + (RY, 128), BF16)] * 6
     scratch += [vm(chunk + (RY, 128), F32), vm((NVOC, RY, 256), F32)]
@@ -526,15 +543,15 @@
     scratch += [vm((2, RV, T), F32)] * 2
     scratch += [vm((RV, T), BF16)] * 2
     scratch += [pltpu.SMEM((NBLK,), jnp.int32)] * 3
-    scratch += [dma((3,)), dma((4,)), dma((4,)), dma((NVOC,)), dma((NVOC,)), dma(()), dma(())]
+    scratch += [dma((2,)), dma((4,)), dma((4,)), dma((4,)), dma((NVOC,)), dma((NVOC,)), dma(()), dma(())]
     scratch += [dma((NVOC,))] * 4
     scratch += [dma(chunk)] * 6 + [dma((NVOC,))] * 6 + [dma((2,))] * 6 + [dma(())] * 2
     anywhere = pl.BlockSpec(memory_space=pl.ANY)
     in_vmem = pl.BlockSpec(memory_space=pltpu.VMEM)
-    return pl.pallas_call(
+    d_hidden, d_head = pl.pallas_call(
         kernel,
         out_shape=(
-            jax.ShapeDtypeStruct((T, RV), BF16),
+            jax.ShapeDtypeStruct((RV, T), BF16),
             jax.ShapeDtypeStruct((R, V), F32),
         ),
         in_specs=[pl.BlockSpec(memory_space=pltpu.SMEM), in_vmem, anywhere, anywhere, anywhere],
@@ -543,7 +560,8 @@
         compiler_params=pltpu.CompilerParams(
             collective_id=0, has_side_effects=True, vmem_limit_bytes=63 * 2**20
         ),
-    )(slot_blocks, segment_ids.reshape(1, T), hidden, head, teacher_logp)
+    )(slot_blocks, segment_ids, hidden, head.T, teacher_logp.T)
+    return d_hidden.T, d_head
 
 
 def solution(mesh):

time: 113 us -> 86.3 us (0.76)
  local copies, waits for them, and re-layouts: 20.3 us -> 3.56 us
  Pallas kernels: 91.4 us -> 82 us
    unnamed x3 -> x2, local copies, waits for them, and re-layouts: 17.3 us -> 3.56 us
    pallas_call x1, Pallas kernels: 91.4 us -> 82 us  [body(): pl.pallas_call(kernel, out_shape=(jax.ShapeDtypeStruct((RV, T), BF16), ja...]
    pallas_call x1 -> x0, local copies, waits for them, and re-layouts: 1.79 us -> none  [body(): pl.pallas_call(kernel, out_shape=(jax.ShapeDtypeStruct((T, RV), BF16), ja...]
    reshape x1 -> x0, local copies, waits for them, and re-layouts: 1.25 us -> none  [body(): segment_ids.reshape(1, T)]
where the time goes in v2:
time: 86.3 us; the launch traced here: 86.2 us
  Pallas kernels  82 us (95%)
  local copies, waits for them, and re-layouts  3.56 us (4%)
    pallas_call x1, Pallas kernels, body(): pl.pallas_call(kernel, out_shape=(jax.ShapeDtypeStruct((RV, T), BF16), ja...  82 us
    unnamed x2, local copies, waits for them, and re-layouts  3.56 us

profile of v2, /device:TPU:1, one launch (start us, length us, event | category | flops | bytes accessed | tf_op | source)
XLA Modules:
  0.0 86.2 jit_solution(12183945172993969405)
XLA Ops:
  0.6 82.0 %shard_map.68 = (bf16[288,384]{1,0:T(8,128)(2,1)}, f32[72,2000]{1,0:T(8,128)}) custom-call(s32[128]{0:T(128)} %slot.1, s32[384]{0:T(512)} %seg.1, bf16[384,2304]{1,0:T(8,128)(2,1)} %hid_h.1, bf16[2000,2304]{1,0:T(8,128)(2,1)} %bitcast.3, bf16[2000,384]{1,0:T(8,128)(2,1)} %bitcast.4), custom_call_target="tpu_custom_call" | custom-call | tf_op jit(solution)/shard_map/pallas_call | solution.py:551
  82.6 1.6 %copy.9 = bf16[384,288]{0,1:T(8,128)(2,1)} copy(bf16[384,288]{0,1:T(8,128)(2,1)} %bitcast.5) | data formatting | bytes 442368
  84.2 1.9 %copy.10 = f32[72,2000]{1,0:T(8,128)} copy(f32[72,2000]{1,0:T(8,128)} %get-tuple-element.9) | data formatting | bytes 1152000

commit v3 on v2

--- a/solution.py
+++ b/solution.py
@@ -137,18 +137,21 @@
 
     total_part = jnp.zeros((8, T), F32)
     valid = lax.broadcasted_iota(jnp.int32, (128, T), 0) < BC
-    for b in range(NBLK):
-        if b % 4 == 0:
-            head_copy(b // 4).wait()
-            if b < 8:
-                head_copy(b // 4 + 2).start()
-        nat32[b * 128 : b * 128 + 128, :] = dot(head_v[b * 128 : b * 128 + 128, :], htn[...])
-        th = jnp.tanh(nat32[b * BC : b * BC + 128, :] * (1.0 / CAP))
-        shifted = jnp.exp(CAP * th - CAP)
-        slope = 1.0 - th * th
-        pblk[b] = shifted * slope
-        qblk[b] = slope
-        total_part += fold(jnp.where(valid, shifted, 0.0))
+    for p in range(5):
+        if p < 4:
+            head_copy(p).wait()
+            if p < 2:
+                head_copy(p + 2).start()
+            nat32[p * 512 : p * 512 + 512, :] = dot(head_v[p * 512 : p * 512 + 512, :], htn[...])
+        for b in range(4 * p - 4, 4 * p):
+            if b < 0:
+                continue
+            th = jnp.tanh(nat32[b * BC : b * BC + 128, :] * (1.0 / CAP))
+            shifted = jnp.exp(CAP * th - CAP)
+            slope = 1.0 - th * th
+            pblk[b] = shifted * slope
+            qblk[b] = slope
+            total_part += fold(jnp.where(valid, shifted, 0.0))
 
     sub = lax.broadcasted_iota(jnp.int32, (8, T), 0)
     total_row = jnp.sum(total_part, axis=0, keepdims=True)
@@ -399,10 +402,12 @@
         hm(0, 3)
 
     def h0():
-        hm(3, 9)
+        hm(6, 9)
         for h in range(2):
             xfar_s[h] = part_h(2, h).astype(BF16)
             xfar(h).start()
+
+    def hd():
         xdir_s[1] = part_h(1, 1).astype(BF16)
         xdir(1).start()
         xdir_s[0] = part_h(3, 0).astype(BF16)
@@ -462,7 +467,9 @@
         stage(c3, LAG_C3)
         stage(c4, LAG_C4)
         pl.when(n == TICK_H)(ha)
-        pl.when(n == TICK_H + 1)(h0)
+        pl.when(n == TICK_H + 1)(lambda: hm(3, 6))
+        pl.when(n == TICK_H + 2)(h0)
+        pl.when(n == TICK_H + 3)(hd)
         pl.when(n == TICK_H + 3)(h1)
         pl.when(n == TICK_H + 6)(h2)
         pl.when(n == TICK_H + 8)(h3)

time: 86.3 us -> 84.5 us (0.979)
  the two profiles are of different devices: /device:TPU:1 before, /device:TPU:34 now
where the time goes in v3:
time: 84.5 us; the launch traced here: 84.4 us
  Pallas kernels  80.2 us (95%)
  local copies, waits for them, and re-layouts  3.56 us (4%)
    pallas_call x1, Pallas kernels, body(): pl.pallas_call(kernel, out_shape=(jax.ShapeDtypeStruct((RV, T), BF16), ja...  80.2 us
    unnamed x2, local copies, waits for them, and re-layouts  3.56 us

profile of v3, /device:TPU:34, one launch (start us, length us, event | category | flops | bytes accessed | tf_op | source)
XLA Modules:
  0.0 84.4 jit_solution(7791350229626169695)
XLA Ops:
  0.6 80.2 %shard_map.68 = (bf16[288,384]{1,0:T(8,128)(2,1)}, f32[72,2000]{1,0:T(8,128)}) custom-call(s32[128]{0:T(128)} %slot.1, s32[384]{0:T(512)} %seg.1, bf16[384,2304]{1,0:T(8,128)(2,1)} %hid_h.1, bf16[2000,2304]{1,0:T(8,128)(2,1)} %bitcast.3, bf16[2000,384]{1,0:T(8,128)(2,1)} %bitcast.4), custom_call_target="tpu_custom_call" | custom-call | tf_op jit(solution)/shard_map/pallas_call | solution.py:558
  80.8 1.6 %copy.9 = bf16[384,288]{0,1:T(8,128)(2,1)} copy(bf16[384,288]{0,1:T(8,128)(2,1)} %bitcast.5) | data formatting | bytes 442368
  82.4 1.9 %copy.10 = f32[72,2000]{1,0:T(8,128)} copy(f32[72,2000]{1,0:T(8,128)} %get-tuple-element.9) | data formatting | bytes 1152000

commit v4 on v3

--- a/solution.py
+++ b/solution.py
@@ -45,13 +45,13 @@
 
 
 def kernel(
-    slot, seg, hid_h, head_h, tea_h, dhid_o, dhead_o,
+    slot, seg, hid_h, head_h, tea_h, dhid_o, fin, inv,
     tea_v, hid_v, head_v, tea32, nat32, tblk, tsend, trec, idb, h32, htn, hsend, ht,
     pblk, qblk, tots, arow, wrow, gc, gslot, gnat,
     yfar_s, yfar_r, ydir_s, ydir_r, yst_s, yst_r, ymid, yown,
-    zfar_s, zfar_r, zdir_s, zdir_r, zst_s, zst_r, fin,
+    zfar_s, zfar_r, zdir_s, zdir_r, zst_s, zst_r,
     xfar_s, xfar_r, xdir_s, xdir_r, xst_s, xst_r, xmid, xown, zl_s, zl_r,
-    snd, blk, inv,
+    snd, blk,
     lsem, hd_sem, id_ss, id_rs, t_ss, t_rs, ht_ss, ht_rs, tot_ss, tot_rs, g_ss, g_rs,
     yfar_ss, yfar_rs, ydir_ss, ydir_rs, yst_ss, yst_rs,
     zfar_ss, zfar_rs, zdir_ss, zdir_rs, zst_ss, zst_rs,
@@ -474,22 +474,6 @@
         pl.when(n == TICK_H + 6)(h2)
         pl.when(n == TICK_H + 8)(h3)
 
-    lane = lax.broadcasted_iota(jnp.int32, (R, 128), 1)
-
-    def rolled_out(b):
-        block = fin[inv[b]]
-        return pltpu.roll(block, 128 - 3 * b, 1) if b else block
-
-    here = rolled_out(0)
-    for q in range(NBLK):
-        after = rolled_out(q + 1) if q < 15 else here
-        tile = jnp.where(lane < BC - 3 * q, here, after)
-        if q < 15:
-            dhead_o[:, q * 128 : q * 128 + 128] = tile
-        else:
-            dhead_o[:, 1920:V] = tile[:, 0:LAST]
-        here = after
-
     for i in range(4):
         id_send(i).wait_send()
     for d in range(1, NVOC):
@@ -513,6 +497,25 @@
         xdir(h).wait_send()
         xst(h).wait_send()
     zlx.wait_send()
+
+
+def finish(inv, fin, dhid, dhid_o, dhead_o):
+    lane = lax.broadcasted_iota(jnp.int32, (R, 128), 1)
+
+    def rolled_out(b):
+        block = fin[inv[b]]
+        return pltpu.roll(block, 128 - 3 * b, 1) if b else block
+
+    here = rolled_out(0)
+    for q in range(NBLK):
+        after = rolled_out(q + 1) if q < 15 else here
+        tile = jnp.where(lane < BC - 3 * q, here, after)
+        if q < 15:
+            dhead_o[:, q * 128 : q * 128 + 128] = tile
+        else:
+            dhead_o[:, 1920:V] = tile[:, 0:LAST]
+        here = after
+    dhid_o[...] = dhid[...]
 
 
 def body(hidden, head, teacher_logp, slot_blocks, segment_ids):
@@ -545,29 +548,35 @@
     scratch += [vm(chunk + (RY, 128), BF16)] * 6
     scratch += [vm(chunk + (RY, 128), F32), vm((NVOC, RY, 256), F32)]
     scratch += [vm((NVOC, 2 * R, 128), BF16)] * 6
-    scratch += [vm((NBLK, R, 128), F32)]
     scratch += [vm((2, RV, T), BF16)] * 6
     scratch += [vm((2, RV, T), F32)] * 2
     scratch += [vm((RV, T), BF16)] * 2
-    scratch += [pltpu.SMEM((NBLK,), jnp.int32)] * 3
+    scratch += [pltpu.SMEM((NBLK,), jnp.int32)] * 2
     scratch += [dma((2,)), dma((4,)), dma((4,)), dma((4,)), dma((NVOC,)), dma((NVOC,)), dma(()), dma(())]
     scratch += [dma((NVOC,))] * 4
     scratch += [dma(chunk)] * 6 + [dma((NVOC,))] * 6 + [dma((2,))] * 6 + [dma(())] * 2
     anywhere = pl.BlockSpec(memory_space=pl.ANY)
     in_vmem = pl.BlockSpec(memory_space=pltpu.VMEM)
-    d_hidden, d_head = pl.pallas_call(
+    d_hidden, blocks, inv = pl.pallas_call(
         kernel,
         out_shape=(
             jax.ShapeDtypeStruct((RV, T), BF16),
-            jax.ShapeDtypeStruct((R, V), F32),
+            jax.ShapeDtypeStruct((NBLK, R, 128), F32),
+            jax.ShapeDtypeStruct((NBLK,), jnp.int32),
         ),
         in_specs=[pl.BlockSpec(memory_space=pltpu.SMEM), in_vmem, anywhere, anywhere, anywhere],
-        out_specs=(in_vmem, in_vmem),
+        out_specs=(in_vmem, in_vmem, pl.BlockSpec(memory_space=pltpu.SMEM)),
         scratch_shapes=scratch,
         compiler_params=pltpu.CompilerParams(
             collective_id=0, has_side_effects=True, vmem_limit_bytes=63 * 2**20
         ),
     )(slot_blocks, segment_ids, hidden, head.T, teacher_logp.T)
+    d_hidden, d_head = pl.pallas_call(
+        finish,
+        out_shape=(jax.ShapeDtypeStruct((RV, T), BF16), jax.ShapeDtypeStruct((R, V), F32)),
+        in_specs=[pl.BlockSpec(memory_space=pltpu.SMEM), in_vmem, in_vmem],
+        out_specs=(in_vmem, in_vmem),
+    )(inv, blocks, d_hidden)
     return d_hidden.T, d_head
 
 

time: 84.5 us -> 82.9 us (0.981)
  local copies, waits for them, and re-layouts: 3.56 us -> 0 us
  Pallas kernels: 80.2 us -> 82.1 us
    unnamed x2 -> x0, local copies, waits for them, and re-layouts: 3.56 us -> none
    pallas_call x0 -> x1, Pallas kernels: none -> 2.18 us  [body(): pl.pallas_call(finish, out_shape=(jax.ShapeDtypeStruct((RV, T), BF16), ja...]
where the time goes in v4:
time: 82.9 us; the launch traced here: 82.8 us
  Pallas kernels  82.1 us (99%)
    pallas_call x1, Pallas kernels, body(): pl.pallas_call(kernel, out_shape=(jax.ShapeDtypeStruct((RV, T), BF16), ja...  80 us
    pallas_call x1, Pallas kernels, body(): pl.pallas_call(finish, out_shape=(jax.ShapeDtypeStruct((RV, T), BF16), ja...  2.18 us

profile of v4, /device:TPU:34, one launch (start us, length us, event | category | flops | bytes accessed | tf_op | source)
XLA Modules:
  0.0 82.8 jit_solution(4731662088034570806)
XLA Ops:
  0.6 80.0 %shard_map.68 = (bf16[288,384]{1,0:T(8,128)(2,1)}, f32[16,72,128]{2,1,0:T(8,128)}, s32[16]{0:T(128)}) custom-call(s32[128]{0:T(128)} %slot.1, s32[384]{0:T(512)} %seg.1, bf16[384,2304]{1,0:T(8,128)(2,1)} %hid_h.1, bf16[2000,2304]{1,0:T(8,128)(2,1)} %bitcast.3, bf16[2000,384]{1,0:T(8,128)(2,1)} %bitcast.4), custom_call_target="tpu_custom_call" | custom-call | tf_op jit(solution)/shard_map/pallas_call | solution.py:560
  80.6 2.2 %shard_map.69 = (bf16[288,384]{1,0:T(8,128)(2,1)}, f32[72,2000]{1,0:T(8,128)}) custom-call(s32[16]{0:T(128)} %get-tuple-element.7.inv, f32[16,72,128]{2,1,0:T(8,128)} %get-tuple-element.8.fin, bf16[288,384]{1,0:T(8,128)(2,1)} %get-tuple-element.9.dhid), custom_call_target="tpu_custom_call" | custom-call | tf_op jit(solution)/shard_map/pallas_call | solution.py:574

commit v5 on v4

--- a/solution.py
+++ b/solution.py
@@ -126,6 +126,46 @@
     mass_part = lax.fori_loop(0, V // 80, tea_step, jnp.zeros((8, T), F32))
     tea32[V:VP, :] = jnp.zeros((VP - V, T), F32)
 
+    def offset(k):
+        out = jnp.int32(0)
+        for i in range(1, NVOC):
+            out = jnp.where(k == i, ORDER[i], out)
+        return out
+
+    @pl.loop(0, NVOC)
+    def _(d):
+        low = lax.rem(v + NVOC - offset(d), NVOC) * NBLK
+        first = jnp.int32(0)
+        last = jnp.int32(0)
+        for j in range(NBLK):
+            e = slot[v * NBLK + j]
+            last = jnp.where((e >= low) & (e < low + NBLK), j, last)
+            e = slot[v * NBLK + NBLK - 1 - j]
+            first = jnp.where((e >= low) & (e < low + NBLK), NBLK - 1 - j, first)
+        snd[2 * d] = first
+        snd[2 * d + 1] = last
+
+    @pl.loop(0, NVOC)
+    def _(k):
+        base = lax.rem(v + offset(k), NVOC) * NBLK
+        low = v * NBLK
+        first = jnp.int32(0)
+        last = jnp.int32(0)
+        for j in range(NBLK):
+            e = slot[base + j]
+            last = jnp.where((e >= low) & (e < low + NBLK), e - low, last)
+            e = slot[base + NBLK - 1 - j]
+            first = jnp.where((e >= low) & (e < low + NBLK), e - low, first)
+        blk[2 * k] = first
+        blk[2 * k + 1] = last
+
+    @pl.loop(0, NBLK)
+    def _(b):
+        place = jnp.int32(0)
+        for s in range(NBLK):
+            place = jnp.where(blk[s] == b, s, place)
+        inv[b] = place
+
     hid_copy.wait()
 
     @pl.loop(0, D // 128)
@@ -192,25 +232,6 @@
     def _(yy):
         ht[yy, :, 0:T] = pack(c, yy)
 
-    def offset(k):
-        out = jnp.int32(0)
-        for i in range(1, NVOC):
-            out = jnp.where(k == i, ORDER[i], out)
-        return out
-
-    @pl.loop(0, NVOC)
-    def _(d):
-        low = lax.rem(v + NVOC - offset(d), NVOC) * NBLK
-        first = jnp.int32(0)
-        last = jnp.int32(0)
-        for j in range(NBLK):
-            e = slot[v * NBLK + j]
-            last = jnp.where((e >= low) & (e < low + NBLK), j, last)
-            e = slot[v * NBLK + NBLK - 1 - j]
-            first = jnp.where((e >= low) & (e < low + NBLK), NBLK - 1 - j, first)
-        snd[2 * d] = first
-        snd[2 * d + 1] = last
-
     for b in range(NBLK):
         tblk[b] = tea32[b * BC : b * BC + 128, :].astype(BF16)
 
@@ -221,27 +242,6 @@
 
     for k in range(1, AHEAD):
         tea_send(k).start()
-
-    @pl.loop(0, NVOC)
-    def _(k):
-        base = lax.rem(v + offset(k), NVOC) * NBLK
-        low = v * NBLK
-        first = jnp.int32(0)
-        last = jnp.int32(0)
-        for j in range(NBLK):
-            e = slot[base + j]
-            last = jnp.where((e >= low) & (e < low + NBLK), e - low, last)
-            e = slot[base + NBLK - 1 - j]
-            first = jnp.where((e >= low) & (e < low + NBLK), e - low, first)
-        blk[2 * k] = first
-        blk[2 * k + 1] = last
-
-    @pl.loop(0, NBLK)
-    def _(b):
-        place = jnp.int32(0)
-        for s in range(NBLK):
-            place = jnp.where(blk[s] == b, s, place)
-        inv[b] = place
 
     for i in range(4):
         id_send(i).wait_recv()

time: 82.9 us -> 84.6 us (1.021)
  Pallas kernels: 82.1 us -> 83.2 us
    pallas_call x1, Pallas kernels: 80 us -> 81 us  [body(): pl.pallas_call(kernel, out_shape=(jax.ShapeDtypeStruct((RV, T), BF16), ja...]
where the time goes in v5:
time: 84.6 us; the launch traced here: 83.9 us
  Pallas kernels  83.2 us (98%)
    pallas_call x1, Pallas kernels, body(): pl.pallas_call(kernel, out_shape=(jax.ShapeDtypeStruct((RV, T), BF16), ja...  81 us
    pallas_call x1, Pallas kernels, body(): pl.pallas_call(finish, out_shape=(jax.ShapeDtypeStruct((RV, T), BF16), ja...  2.17 us

profile of v5, /device:TPU:34, one launch (start us, length us, event | category | flops | bytes accessed | tf_op | source)
XLA Modules:
  0.0 83.9 jit_solution(1995704644132751835)
XLA Ops:
  0.6 81.0 %shard_map.68 = (bf16[288,384]{1,0:T(8,128)(2,1)}, f32[16,72,128]{2,1,0:T(8,128)}, s32[16]{0:T(128)}) custom-call(s32[128]{0:T(128)} %slot.1, s32[384]{0:T(512)} %seg.1, bf16[384,2304]{1,0:T(8,128)(2,1)} %hid_h.1, bf16[2000,2304]{1,0:T(8,128)(2,1)} %bitcast.3, bf16[2000,384]{1,0:T(8,128)(2,1)} %bitcast.4), custom_call_target="tpu_custom_call" | custom-call | tf_op jit(solution)/shard_map/pallas_call | solution.py:560
  81.7 2.2 %shard_map.69 = (bf16[288,384]{1,0:T(8,128)(2,1)}, f32[72,2000]{1,0:T(8,128)}) custom-call(s32[16]{0:T(128)} %get-tuple-element.7.inv, f32[16,72,128]{2,1,0:T(8,128)} %get-tuple-element.8.fin, bf16[288,384]{1,0:T(8,128)(2,1)} %get-tuple-element.9.dhid), custom_call_target="tpu_custom_call" | custom-call | tf_op jit(solution)/shard_map/pallas_call | solution.py:574
